TPU v7x, 256 devices: a whole 4x4x8 slice. The times are simulated.
256 devices in a mesh: stn: 16 (over z, x_hi), tf: 16 (over y, x_lo, core).
Axes of the slice: x: 4 (x_hi: 2, x_lo: 2; x = x_hi * 2 + x_lo), y: 4, z: 8, core: 2. Of those that a mesh axis runs over, the one named last changes fastest.
Arguments:
- voltages: bfloat16 [2, 128, 2, 524288], P(None, 'stn', None, 'tf'), may hold values from -6 to 6
- delay_table: float32 [128, 128], replicated, may hold values from -512 to 512
- beam_pointing: int32 [32], replicated, may hold values from 0 to 127
- station_group: int32 [128], replicated, may hold values from 0 to 3
Outputs:
- beams: bfloat16 [32, 2, 2, 128, 32, 128], P('stn', None, None, None, 'tf')
All inputs are finite; a program needn't handle non-finite values.
Results may differ from a plain program's by a relative error of at most 0.0082.
Values may be sent and summed in bfloat16 or wider, within the bound.
A program may use at most 128 MiB of HBM per device.

v0:
```python
import math

import jax
import jax.numpy as jnp
import numpy as np
from jax import lax
from jax.experimental import pallas as pl
from jax.experimental.pallas import tpu as pltpu
from jax.sharding import PartitionSpec as P

TAPS = 16
CH_LO = 32
CH_HI = 128
POINTS = CH_LO * CH_HI
GROUPS = 4
TWO_PI = 2.0 * math.pi
BF = jnp.bfloat16
F32 = jnp.float32
MESH = pl.DeviceIdType.MESH

N = 16
FRAMES_OWN = 8
STEPS = 8
BB = 8


def filter_window():
    position = jnp.arange(TAPS * POINTS, dtype=jnp.int32).astype(F32)
    total = float(TAPS * POINTS)
    taper = 0.5 - 0.5 * jnp.cos(TWO_PI / total * position)
    kernel = jnp.sinc((position - 0.5 * total) / float(POINTS)) * taper
    return kernel.reshape(TAPS, CH_LO, CH_HI)


def dft_table(points):
    counter = np.arange(points)
    angles = 2.0 * np.pi / points * (counter[:, None] * counter[None, :] % points)
    cosine = np.cos(angles) / math.sqrt(points)
    sine = np.sin(angles) / math.sqrt(points)
    return np.stack([np.stack([cosine, sine]), np.stack([-sine, cosine])])


def low_matrix():
    table = dft_table(CH_LO)
    eye = np.eye(8)
    full = np.einsum("oqkn,fg->kofgqn", table, eye)
    return jnp.asarray(full.reshape(512, 512).astype(np.float32)).astype(BF)


def high_matrix():
    table = dft_table(CH_HI)
    return jnp.asarray(
        table.transpose(1, 2, 0, 3).reshape(256, 256).astype(np.float32)
    ).astype(BF)


def twiddle_table():
    angle = 2.0 * np.pi / POINTS * (np.arange(CH_LO)[:, None] * np.arange(CH_HI)[None, :])
    pair = np.stack([np.cos(angle), np.sin(angle)], axis=1)
    return jnp.asarray(np.concatenate([pair, pair], axis=-1).astype(np.float32))


def turn_parts(turns):
    t = (turns - jnp.round(turns)) * math.pi
    y = t * t
    s = t * (
        1.0
        + y
        * (
            -1.0 / 6
            + y
            * (
                1.0 / 120
                + y * (-1.0 / 5040 + y * (1.0 / 362880 + y * (-1.0 / 39916800 + y / 6227020800.0)))
            )
        )
    )
    c = 1.0 + y * (
        -0.5
        + y
        * (
            1.0 / 24
            + y
            * (
                -1.0 / 720
                + y * (1.0 / 40320 + y * (-1.0 / 3628800 + y * (1.0 / 479001600)))
            )
        )
    )
    return 1.0 - 2.0 * s * s, 2.0 * s * c


def z_shift(step):
    k = 7 - step
    half = (k + 1) // 2
    return half * (2 * (k % 2) - 1)


def fused(
    xv, win, low, high, twid, delay, member,
    out,
    rbuf, filt, chan, recv, weights, acc, csend,
    send_a, recv_a, send_b, recv_b, send_c, recv_c,
):
    i = lax.axis_index("stn")
    j = lax.axis_index("tf")
    z = i // 2
    parity = j % 2

    own_a = pltpu.make_async_copy(xv.at[j], rbuf.at[pl.ds(16 + 8 * j, 8)], recv_a)
    own_a.start()

    def send_voltages(step, carry):
        target = lax.rem(j + step, N)
        pltpu.make_async_remote_copy(
            src_ref=xv.at[target],
            dst_ref=rbuf.at[pl.ds(16 + 8 * j, 8)],
            send_sem=send_a,
            recv_sem=recv_a,
            device_id=(i, target),
            device_id_type=MESH,
        ).start()
        return carry

    lax.fori_loop(1, N, send_voltages, 0)

    rbuf[pl.ds(0, 16)] = jnp.zeros((16, 2, CH_LO, CH_HI), BF)
    acc[...] = jnp.zeros(acc.shape, F32)

    lane = lax.broadcasted_iota(jnp.int32, (8, CH_HI), 1)
    lane4 = lax.broadcasted_iota(jnp.int32, (GROUPS, CH_HI), 1)

    def make_weights(s, carry):
        column = jnp.sum(jnp.where(lane == s, delay[...], 0.0), axis=1, keepdims=True)
        scale = jnp.sum(jnp.where(lane4 == s, member[...], 0.0), axis=1, keepdims=True)
        for k2 in range(2):
            channel = (2 * j + k2) + CH_LO * lane
            fraction = channel.astype(F32) * (1.0 / POINTS)
            cosine, sine = turn_parts(column * fraction)
            for g in range(GROUPS):
                amount = scale[g : g + 1, :]
                weights[s, k2, 0, pl.ds(8 * g, 8), :] = (amount * cosine).astype(BF).astype(F32)
                weights[s, k2, 1, pl.ds(8 * g, 8), :] = (amount * -sine).astype(BF).astype(F32)
        return carry

    lax.fori_loop(0, 128, make_weights, 0)

    pltpu.make_async_copy(rbuf.at[pl.ds(16, 128)], rbuf.at[pl.ds(16, 128)], recv_a).wait()

    def block(step, carry):
        fb = lax.rem(z + z_shift(step) + 8, 8)
        i_to = 2 * fb + parity

        def filter_part(part, inner):
            q = part // 2
            row = pl.multiple_of((part % 2) * 16, 16)
            for g2 in range(2):
                base = fb * 16 + g2 * 8
                sums = [None] * 8
                taps = [win[t, pl.ds(row, 16), :] for t in range(TAPS)]
                for k in range(1, 24):
                    x = rbuf[base + k, q, pl.ds(row, 16), :].astype(F32)
                    for f in range(8):
                        t = k - 1 - f
                        if 0 <= t < TAPS:
                            term = taps[t] * x
                            sums[f] = term if sums[f] is None else sums[f] + term
                for f in range(8):
                    filt[pl.ds(pl.multiple_of(f * 64 + q * 32 + row, 16), 16), pl.ds(128 * g2, 128)] = sums[f].astype(BF)
            return inner

        lax.fori_loop(0, 4, filter_part, 0)

        def transform(part, inner):
            c = lax.rem(part + j // 4, 4)
            first = jnp.dot(
                low[pl.ds(pl.multiple_of(c * 128, 128), 128), :], filt[...], preferred_element_type=F32
            ).reshape(8, 2, 8, 256)
            table = twid[pl.ds(c * 8, 8)]
            cosine, sine = table[:, 0:1, :], table[:, 1:2, :]
            re = first[:, 0] * cosine + first[:, 1] * sine
            im = first[:, 1] * cosine - first[:, 0] * sine
            re = jnp.concatenate([re[:, :, :128], re[:, :, 128:]], axis=1).astype(BF)
            im = jnp.concatenate([im[:, :, :128], im[:, :, 128:]], axis=1).astype(BF)
            rotated = jnp.concatenate([re, im], axis=2).reshape(128, 256)
            done = jnp.dot(rotated, high[...], preferred_element_type=F32).astype(BF)
            chan[step, pl.ds(c * 8, 8)] = done.reshape(8, 16, 256)

            def send(n, deep):
                j_to = c * 4 + lax.rem(n + j, 4)
                here = jnp.logical_and(i_to == i, j_to == j)
                source = chan.at[step, pl.ds(2 * j_to, 2)]
                target = recv.at[8 * i + j // 2]

                @pl.when(here)
                def _():
                    pltpu.make_async_copy(source, target, recv_b.at[i]).start()

                @pl.when(jnp.logical_not(here))
                def _():
                    pltpu.make_async_remote_copy(
                        src_ref=source,
                        dst_ref=target,
                        send_sem=send_b.at[step],
                        recv_sem=recv_b.at[i],
                        device_id=(i_to, j_to),
                        device_id_type=MESH,
                    ).start()

                return deep

            lax.fori_loop(0, 4, send, 0)
            return inner

        lax.fori_loop(0, 4, transform, 0)
        return carry

    lax.fori_loop(0, STEPS, block, 0)

    def add_block(step, carry):
        z_from = lax.rem(z - z_shift(step // 2) + 8, 8)
        i_from = 2 * z_from + step % 2
        s0 = 8 * i_from
        pltpu.make_async_copy(recv.at[pl.ds(s0, 8)], recv.at[pl.ds(s0, 8)], recv_b.at[i_from]).wait()

        def part(n, inner):
            k2 = n // 4
            g = n % 4
            re = [acc[k2, g, b, 0] for b in range(BB)]
            im = [acc[k2, g, b, 1] for b in range(BB)]
            for s in range(8):
                value = recv[s0 + s, k2].astype(F32)
                vr, vi = value[:, :128], value[:, 128:]
                for b in range(BB):
                    wr = weights[s0 + s, k2, 0, pl.ds(8 * g + b, 1), :]
                    wi = weights[s0 + s, k2, 1, pl.ds(8 * g + b, 1), :]
                    re[b] = re[b] + (wr * vr - wi * vi)
                    im[b] = im[b] + (wr * vi + wi * vr)
            for b in range(BB):
                acc[k2, g, b, 0] = re[b]
                acc[k2, g, b, 1] = im[b]
            return inner

        lax.fori_loop(0, 8, part, 0)
        return carry

    lax.fori_loop(0, N, add_block, 0)

    for k2 in range(2):
        for g in range(GROUPS):
            for b in range(BB):
                for q in range(2):
                    csend[2 * b + g // 2, g % 2, q, k2] = acc[k2, g, b, q].astype(BF)

    own_c = pltpu.make_async_copy(csend.at[i], out.at[i], recv_c)
    own_c.start()

    def send_beams(step, carry):
        target = lax.rem(i + step, N)
        pltpu.make_async_remote_copy(
            src_ref=csend.at[target],
            dst_ref=out.at[i],
            send_sem=send_c,
            recv_sem=recv_c,
            device_id=(target, j),
            device_id_type=MESH,
        ).start()
        return carry

    lax.fori_loop(1, N, send_beams, 0)

    pltpu.make_async_copy(rbuf.at[pl.ds(0, 120)], rbuf.at[pl.ds(0, 120)], send_a).wait()

    def wait_sent(step, carry):
        fb = lax.rem(z + z_shift(step) + 8, 8)
        mine = jnp.logical_and(2 * fb + parity == i, True)

        @pl.when(mine)
        def _():
            pltpu.make_async_copy(
                chan.at[step, pl.ds(0, 30)], chan.at[step, pl.ds(0, 30)], send_b.at[step]
            ).wait()

        @pl.when(jnp.logical_not(mine))
        def _():
            pltpu.make_async_copy(chan.at[step], chan.at[step], send_b.at[step]).wait()

        return carry

    lax.fori_loop(0, STEPS, wait_sent, 0)
    pltpu.make_async_copy(csend.at[pl.ds(0, 15)], csend.at[pl.ds(0, 15)], send_c).wait()
    pltpu.make_async_copy(csend, csend, recv_c).wait()


def body(voltages, delay_table, beam_pointing, station_group):
    stations_here = voltages.shape[1]
    parts = voltages.reshape(2, stations_here, 2, FRAMES_OWN, CH_LO, CH_HI)
    xv = parts.transpose(1, 2, 3, 0, 4, 5).reshape(N, FRAMES_OWN, 2, CH_LO, CH_HI)

    stations = station_group.shape[0]
    delays = jnp.take(delay_table, beam_pointing, axis=0, mode="clip")
    delays = delays.reshape(BB, GROUPS, stations)
    groups = jnp.arange(GROUPS, dtype=jnp.int32)
    own = station_group[None, :] == groups[:, None]
    delay = jnp.sum(jnp.where(own[None], delays, 0.0), axis=1)
    member = math.sqrt(GROUPS / stations) * own.astype(F32)

    vmem = pl.BlockSpec(memory_space=pltpu.VMEM)
    anywhere = pl.BlockSpec(memory_space=pl.ANY)
    out = pl.pallas_call(
        fused,
        out_shape=jax.ShapeDtypeStruct((N, 2, 2, 2, 16, CH_HI), BF),
        in_specs=[anywhere] + [vmem] * 6,
        out_specs=anywhere,
        scratch_shapes=[
            pltpu.VMEM((144, 2, CH_LO, CH_HI), BF),
            pltpu.VMEM((512, 256), BF),
            pltpu.VMEM((STEPS, CH_LO, 16, 256), BF),
            pltpu.VMEM((128, 2, 16, 256), BF),
            pltpu.VMEM((128, 2, 2, 32, CH_HI), F32),
            pltpu.VMEM((2, GROUPS, BB, 2, 16, CH_HI), F32),
            pltpu.VMEM((N, 2, 2, 2, 16, CH_HI), BF),
            pltpu.SemaphoreType.DMA,
            pltpu.SemaphoreType.DMA,
            pltpu.SemaphoreType.DMA((STEPS,)),
            pltpu.SemaphoreType.DMA((N,)),
            pltpu.SemaphoreType.DMA,
            pltpu.SemaphoreType.DMA,
        ],
        compiler_params=pltpu.CompilerParams(
            has_side_effects=True, vmem_limit_bytes=40 * 1024 * 1024
        ),
        name="channelize_and_beamform",
    )(xv, filter_window(), low_matrix(), high_matrix(), twiddle_table(), delay, member)

    out = out.reshape(8, 2, 2, 2, 2, 16, CH_HI).transpose(2, 3, 1, 0, 5, 4, 6)
    return out.reshape(2, 2, 2, 128, 2, CH_HI)


def solution(mesh):
    in_specs = (P(None, "stn", None, "tf"), P(), P(), P())
    out_specs = P("stn", None, None, None, "tf", None)
    return jax.shard_map(body, mesh=mesh, in_specs=in_specs, out_specs=out_specs, check_vma=False)
```

profile of v0, /device:TPU:64, one launch (start us, length us, event | category | flops | bytes accessed | tf_op | source)
XLA Modules:
  0.0 123.9 jit_solution(13486319886887366922)
XLA Ops:
  0.0 0.0 copy-start
  0.0 4.5 %reshape.38 = bf16[2,8,2,8,32,128]{5,4,3,2,1,0:T(8,128)(2,1)} reshape(bf16[2,8,2,32768]{3,2,1,0:T(2,128)(2,1)} %param.7) | data formatting | bytes 4194304 | tf_op jit(solution)/shard_map/reshape | solution.py:297
  4.5 0.0 copy-start.4
  4.5 0.0 copy-start.5
  4.5 0.0 copy-start.1
  4.5 0.0 copy-start.2
  4.5 0.0 copy-start.3
  4.5 2.3 %copy.8 = bf16[2,8,2,8,32,128]{5,4,0,3,2,1:T(8,128)(2,1)S(1)} copy(bf16[2,8,2,8,32,128]{5,4,3,2,1,0:T(8,128)(2,1)} %reshape.38) | data formatting | bytes 4194304 | tf_op jit(solution)/shard_map/reshape | solution.py:297
  6.8 1.2 fusion.4.win
  8.0 0.0 copy-done.4
  8.1 0.0 copy-done
  8.1 0.6 gather_fusion
  8.6 0.0 copy-done.5
  8.7 0.0 copy-done.1
  8.7 0.0 copy-done.2
  8.7 0.0 copy-done.3
  8.7 113.9 %channelize_and_beamform.1 = bf16[16,2,2,2,16,128]{5,4,3,2,1,0:T(8,128)(2,1)S(1)} custom-call(bf16[16,8,2,32,128]{4,3,2,1,0:T(8,128)(2,1)S(1)} %bitcast.8, f32[16,32,128]{2,1,0:T(8,128)S(1)} %fusion.4.win, bf16[512,512]{1,0:T(8,128)(2,1)S(1)} %copy-done.1, bf16[256,256]{1,0:T(8,128)(2,1)S(1)} %copy-done.2, f32[32,2,256]{2,1,0:T(2,128)S(1)} %copy-done.3, ...), custom_call_target="tpu_custom_call" | custom-call | tf_op jit(solution)/shard_map/channelize_and_beamform/pallas_call | solution.py:310
  122.7 1.2 %copy.9 = bf16[2,2,2,8,16,2,128]{6,5,4,3,2,1,0:T(2,128)(2,1)} copy(bf16[2,2,2,8,16,2,128]{6,4,5,1,0,2,3:T(8,128)(2,1)S(1)} %bitcast.9) | data formatting | bytes 1048576 | tf_op jit(solution)/shard_map/transpose | solution.py:336
  (4 shorter events, 0.0 us)
Async XLA Ops:
  0.0 8.1 %copy-start = (f32[128,128]{1,0:T(8,128)S(1)}, f32[128,128]{1,0:T(8,128)}, u32[]{:S(2)}) copy-start(f32[128,128]{1,0:T(8,128)} %param.8) | copy-start | bytes 196612
  4.5 3.5 %copy-start.4 = (s32[32]{0:T(128)S(1)}, s32[32]{0:T(128)}, u32[]{:S(2)}) copy-start(s32[32]{0:T(128)} %param.9) | copy-start | bytes 388
  4.5 4.1 %copy-start.5 = (s32[128]{0:T(128)S(1)}, s32[128]{0:T(128)}, u32[]{:S(2)}) copy-start(s32[128]{0:T(128)} %param.10) | copy-start | bytes 1540
  4.5 4.2 %copy-start.1 = (bf16[512,512]{1,0:T(8,128)(2,1)S(1)}, bf16[512,512]{1,0:T(8,128)(2,1)}, u32[]{:S(2)}) copy-start(bf16[512,512]{1,0:T(8,128)(2,1)} %constant.66.low) | copy-start | bytes 1572868
  4.5 4.2 %copy-start.2 = (bf16[256,256]{1,0:T(8,128)(2,1)S(1)}, bf16[256,256]{1,0:T(8,128)(2,1)}, u32[]{:S(2)}) copy-start(bf16[256,256]{1,0:T(8,128)(2,1)} %constant.67.high) | copy-start | bytes 393220
  4.5 4.2 %copy-start.3 = (f32[32,2,256]{2,1,0:T(2,128)S(1)}, f32[32,2,256]{2,1,0:T(2,128)}, u32[]{:S(2)}) copy-start(f32[32,2,256]{2,1,0:T(2,128)} %constant.64.clone.twid) | copy-start | bytes 196612
where the time goes:
time: 124 us
  Pallas kernels  114 us (92%)
  local copies, waits for them, and re-layouts  8.64 us (7%)
    pallas_call x1, Pallas kernels, body(): pl.pallas_call(fused, out_shape=jax.ShapeDtypeStruct((N, 2, 2, 2, 16, CH_...  114 us
    reshape x2, local copies, waits for them, and re-layouts, body(): parts = voltages.reshape(2, stations_here, 2, FRAMES_OWN, CH_LO, CH_HI)  6.8 us

commit v1 on v0

--- a/solution.py
+++ b/solution.py
@@ -25,11 +25,11 @@
 
 
 def filter_window():
-    position = jnp.arange(TAPS * POINTS, dtype=jnp.int32).astype(F32)
+    position = np.arange(TAPS * POINTS, dtype=np.float64)
     total = float(TAPS * POINTS)
-    taper = 0.5 - 0.5 * jnp.cos(TWO_PI / total * position)
-    kernel = jnp.sinc((position - 0.5 * total) / float(POINTS)) * taper
-    return kernel.reshape(TAPS, CH_LO, CH_HI)
+    taper = 0.5 - 0.5 * np.cos(2.0 * np.pi / total * position)
+    kernel = np.sinc((position - 0.5 * total) / POINTS) * taper
+    return jnp.asarray(kernel.reshape(TAPS, CH_LO, CH_HI).astype(np.float32))
 
 
 def dft_table(points):
@@ -97,24 +97,39 @@
 
 
 def fused(
-    xv, win, low, high, twid, delay, member,
+    pointing, xv, win, low, high, twid, table, group,
     out,
-    rbuf, filt, chan, recv, weights, acc, csend,
-    send_a, recv_a, send_b, recv_b, send_c, recv_c,
+    rbuf, filt, first, rotated, chan, recv, delay, weights, acc, csend,
+    entered, send_a, recv_a, send_b, recv_b, send_c, recv_c,
 ):
     i = lax.axis_index("stn")
     j = lax.axis_index("tf")
     z = i // 2
     parity = j % 2
 
-    own_a = pltpu.make_async_copy(xv.at[j], rbuf.at[pl.ds(16 + 8 * j, 8)], recv_a)
+    barrier = pltpu.get_barrier_semaphore()
+
+    def greet(step, carry):
+        pl.semaphore_signal(
+            barrier, inc=1, device_id=(i, lax.rem(j + step, N)), device_id_type=MESH
+        )
+        pl.semaphore_signal(
+            barrier, inc=1, device_id=(lax.rem(i + step, N), j), device_id_type=MESH
+        )
+        return carry
+
+    lax.fori_loop(1, N, greet, 0)
+
+    frames_here = rbuf.at[:, pl.ds(16 + 8 * j, 8)]
+    own_a = pltpu.make_async_copy(xv.at[:, j // 2, parity], frames_here, recv_a)
     own_a.start()
+    pl.semaphore_wait(barrier, 2 * (N - 1))
 
     def send_voltages(step, carry):
         target = lax.rem(j + step, N)
         pltpu.make_async_remote_copy(
-            src_ref=xv.at[target],
-            dst_ref=rbuf.at[pl.ds(16 + 8 * j, 8)],
+            src_ref=xv.at[:, target // 2, lax.rem(target, 2)],
+            dst_ref=frames_here,
             send_sem=send_a,
             recv_sem=recv_a,
             device_id=(i, target),
@@ -124,28 +139,48 @@
 
     lax.fori_loop(1, N, send_voltages, 0)
 
-    rbuf[pl.ds(0, 16)] = jnp.zeros((16, 2, CH_LO, CH_HI), BF)
+    def tell(step, carry):
+        pl.semaphore_signal(
+            entered, inc=1, device_id=(i, lax.rem(j + step, N)), device_id_type=MESH
+        )
+        return carry
+
+    lax.fori_loop(1, N, tell, 0)
+
+    rbuf[:, pl.ds(0, 16)] = jnp.zeros((2, 16, CH_LO, CH_HI), BF)
     acc[...] = jnp.zeros(acc.shape, F32)
 
+    groups = group[...]
+    for b in range(BB):
+        row = jnp.zeros((1, CH_HI), F32)
+        for g in range(GROUPS):
+            row = jnp.where(groups == g, table[pl.ds(pointing[4 * b + g], 1), :], row)
+        delay[pl.ds(b, 1), :] = row
     lane = lax.broadcasted_iota(jnp.int32, (8, CH_HI), 1)
-    lane4 = lax.broadcasted_iota(jnp.int32, (GROUPS, CH_HI), 1)
-
-    def make_weights(s, carry):
-        column = jnp.sum(jnp.where(lane == s, delay[...], 0.0), axis=1, keepdims=True)
-        scale = jnp.sum(jnp.where(lane4 == s, member[...], 0.0), axis=1, keepdims=True)
-        for k2 in range(2):
-            channel = (2 * j + k2) + CH_LO * lane
-            fraction = channel.astype(F32) * (1.0 / POINTS)
-            cosine, sine = turn_parts(column * fraction)
-            for g in range(GROUPS):
-                amount = scale[g : g + 1, :]
-                weights[s, k2, 0, pl.ds(8 * g, 8), :] = (amount * cosine).astype(BF).astype(F32)
-                weights[s, k2, 1, pl.ds(8 * g, 8), :] = (amount * -sine).astype(BF).astype(F32)
-        return carry
-
-    lax.fori_loop(0, 128, make_weights, 0)
-
-    pltpu.make_async_copy(rbuf.at[pl.ds(16, 128)], rbuf.at[pl.ds(16, 128)], recv_a).wait()
+    whose = jnp.broadcast_to(groups, (8, CH_HI))
+
+    def make_weights(part, carry):
+        for more in range(4):
+            s = part * 4 + more
+            here = lane == s
+            column = jnp.sum(jnp.where(here, delay[...], 0.0), axis=1, keepdims=True)
+            mine = jnp.sum(jnp.where(here, whose, 0), axis=1, keepdims=True)
+            for k2 in range(2):
+                channel = (2 * j + k2) + CH_LO * lane
+                fraction = channel.astype(F32) * (1.0 / POINTS)
+                cosine, sine = turn_parts(column * fraction)
+                scale = math.sqrt(GROUPS / 128)
+                cosine = (scale * cosine).astype(BF).astype(F32)
+                sine = (-scale * sine).astype(BF).astype(F32)
+                for g in range(GROUPS):
+                    weights[s, k2, 0, pl.ds(8 * g, 8), :] = jnp.where(mine == g, cosine, 0.0)
+                    weights[s, k2, 1, pl.ds(8 * g, 8), :] = jnp.where(mine == g, sine, 0.0)
+        return carry
+
+    lax.fori_loop(0, 32, make_weights, 0)
+    pl.semaphore_wait(entered, N - 1)
+
+    pltpu.make_async_copy(rbuf.at[:, pl.ds(16, 128)], rbuf.at[:, pl.ds(16, 128)], recv_a).wait()
 
     def block(step, carry):
         fb = lax.rem(z + z_shift(step) + 8, 8)
@@ -159,7 +194,7 @@
                 sums = [None] * 8
                 taps = [win[t, pl.ds(row, 16), :] for t in range(TAPS)]
                 for k in range(1, 24):
-                    x = rbuf[base + k, q, pl.ds(row, 16), :].astype(F32)
+                    x = rbuf[q, base + k, pl.ds(row, 16), :].astype(F32)
                     for f in range(8):
                         t = k - 1 - f
                         if 0 <= t < TAPS:
@@ -171,48 +206,47 @@
 
         lax.fori_loop(0, 4, filter_part, 0)
 
-        def transform(part, inner):
-            c = lax.rem(part + j // 4, 4)
-            first = jnp.dot(
-                low[pl.ds(pl.multiple_of(c * 128, 128), 128), :], filt[...], preferred_element_type=F32
-            ).reshape(8, 2, 8, 256)
-            table = twid[pl.ds(c * 8, 8)]
-            cosine, sine = table[:, 0:1, :], table[:, 1:2, :]
-            re = first[:, 0] * cosine + first[:, 1] * sine
-            im = first[:, 1] * cosine - first[:, 0] * sine
+        first[...] = jnp.dot(low[...], filt[...], preferred_element_type=F32).reshape(32, 2, 8, 256)
+
+        def turn(c, inner):
+            part = pl.ds(c * 8, 8)
+            real, imag = first[part, 0], first[part, 1]
+            cosine, sine = twid[part, 0:1, :], twid[part, 1:2, :]
+            re = real * cosine + imag * sine
+            im = imag * cosine - real * sine
             re = jnp.concatenate([re[:, :, :128], re[:, :, 128:]], axis=1).astype(BF)
             im = jnp.concatenate([im[:, :, :128], im[:, :, 128:]], axis=1).astype(BF)
-            rotated = jnp.concatenate([re, im], axis=2).reshape(128, 256)
-            done = jnp.dot(rotated, high[...], preferred_element_type=F32).astype(BF)
-            chan[step, pl.ds(c * 8, 8)] = done.reshape(8, 16, 256)
-
-            def send(n, deep):
-                j_to = c * 4 + lax.rem(n + j, 4)
-                here = jnp.logical_and(i_to == i, j_to == j)
-                source = chan.at[step, pl.ds(2 * j_to, 2)]
-                target = recv.at[8 * i + j // 2]
-
-                @pl.when(here)
-                def _():
-                    pltpu.make_async_copy(source, target, recv_b.at[i]).start()
-
-                @pl.when(jnp.logical_not(here))
-                def _():
-                    pltpu.make_async_remote_copy(
-                        src_ref=source,
-                        dst_ref=target,
-                        send_sem=send_b.at[step],
-                        recv_sem=recv_b.at[i],
-                        device_id=(i_to, j_to),
-                        device_id_type=MESH,
-                    ).start()
-
-                return deep
-
-            lax.fori_loop(0, 4, send, 0)
+            rotated[part] = jnp.concatenate([re, im], axis=2)
             return inner
 
-        lax.fori_loop(0, 4, transform, 0)
+        lax.fori_loop(0, 4, turn, 0)
+        done = jnp.dot(rotated[...].reshape(512, 256), high[...], preferred_element_type=F32)
+        chan[step] = done.astype(BF).reshape(CH_LO, 16, 256)
+
+        def send(n, inner):
+            j_to = lax.rem(j + n, N)
+            here = jnp.logical_and(i_to == i, j_to == j)
+            source = chan.at[step, pl.ds(2 * j_to, 2)]
+            target = recv.at[8 * i + j // 2]
+
+            @pl.when(here)
+            def _():
+                pltpu.make_async_copy(source, target, recv_b.at[i]).start()
+
+            @pl.when(jnp.logical_not(here))
+            def _():
+                pltpu.make_async_remote_copy(
+                    src_ref=source,
+                    dst_ref=target,
+                    send_sem=send_b.at[step],
+                    recv_sem=recv_b.at[i],
+                    device_id=(i_to, j_to),
+                    device_id_type=MESH,
+                ).start()
+
+            return inner
+
+        lax.fori_loop(0, N, send, 0)
         return carry
 
     lax.fori_loop(0, STEPS, block, 0)
@@ -269,11 +303,11 @@
 
     lax.fori_loop(1, N, send_beams, 0)
 
-    pltpu.make_async_copy(rbuf.at[pl.ds(0, 120)], rbuf.at[pl.ds(0, 120)], send_a).wait()
+    pltpu.make_async_copy(rbuf.at[:, pl.ds(0, 120)], rbuf.at[:, pl.ds(0, 120)], send_a).wait()
 
     def wait_sent(step, carry):
         fb = lax.rem(z + z_shift(step) + 8, 8)
-        mine = jnp.logical_and(2 * fb + parity == i, True)
+        mine = 2 * fb + parity == i
 
         @pl.when(mine)
         def _():
@@ -294,32 +328,27 @@
 
 def body(voltages, delay_table, beam_pointing, station_group):
     stations_here = voltages.shape[1]
-    parts = voltages.reshape(2, stations_here, 2, FRAMES_OWN, CH_LO, CH_HI)
-    xv = parts.transpose(1, 2, 3, 0, 4, 5).reshape(N, FRAMES_OWN, 2, CH_LO, CH_HI)
-
-    stations = station_group.shape[0]
-    delays = jnp.take(delay_table, beam_pointing, axis=0, mode="clip")
-    delays = delays.reshape(BB, GROUPS, stations)
-    groups = jnp.arange(GROUPS, dtype=jnp.int32)
-    own = station_group[None, :] == groups[:, None]
-    delay = jnp.sum(jnp.where(own[None], delays, 0.0), axis=1)
-    member = math.sqrt(GROUPS / stations) * own.astype(F32)
+    xv = voltages.reshape(2, stations_here, 2, FRAMES_OWN, CH_LO, CH_HI)
 
     vmem = pl.BlockSpec(memory_space=pltpu.VMEM)
     anywhere = pl.BlockSpec(memory_space=pl.ANY)
     out = pl.pallas_call(
         fused,
         out_shape=jax.ShapeDtypeStruct((N, 2, 2, 2, 16, CH_HI), BF),
-        in_specs=[anywhere] + [vmem] * 6,
+        in_specs=[pl.BlockSpec(memory_space=pltpu.SMEM), anywhere] + [vmem] * 6,
         out_specs=anywhere,
         scratch_shapes=[
-            pltpu.VMEM((144, 2, CH_LO, CH_HI), BF),
+            pltpu.VMEM((2, 144, CH_LO, CH_HI), BF),
             pltpu.VMEM((512, 256), BF),
+            pltpu.VMEM((CH_LO, 2, 8, 256), F32),
+            pltpu.VMEM((CH_LO, 16, 256), BF),
             pltpu.VMEM((STEPS, CH_LO, 16, 256), BF),
             pltpu.VMEM((128, 2, 16, 256), BF),
+            pltpu.VMEM((8, 128), F32),
             pltpu.VMEM((128, 2, 2, 32, CH_HI), F32),
             pltpu.VMEM((2, GROUPS, BB, 2, 16, CH_HI), F32),
             pltpu.VMEM((N, 2, 2, 2, 16, CH_HI), BF),
+            pltpu.SemaphoreType.REGULAR,
             pltpu.SemaphoreType.DMA,
             pltpu.SemaphoreType.DMA,
             pltpu.SemaphoreType.DMA((STEPS,)),
@@ -328,10 +357,13 @@
             pltpu.SemaphoreType.DMA,
         ],
         compiler_params=pltpu.CompilerParams(
-            has_side_effects=True, vmem_limit_bytes=40 * 1024 * 1024
+            has_side_effects=True, collective_id=0, vmem_limit_bytes=40 * 1024 * 1024
         ),
         name="channelize_and_beamform",
-    )(xv, filter_window(), low_matrix(), high_matrix(), twiddle_table(), delay, member)
+    )(
+        beam_pointing, xv, filter_window(), low_matrix(), high_matrix(), twiddle_table(),
+        delay_table, station_group.reshape(1, -1),
+    )
 
     out = out.reshape(8, 2, 2, 2, 2, 16, CH_HI).transpose(2, 3, 1, 0, 5, 4, 6)
     return out.reshape(2, 2, 2, 128, 2, CH_HI)

time: 124 us -> 113 us (0.911)
  Pallas kernels: 114 us -> 108 us
  local copies, waits for them, and re-layouts: 8.64 us -> 4.68 us
    pallas_call x1, Pallas kernels: 114 us -> 108 us  [body(): pl.pallas_call(fused, out_shape=jax.ShapeDtypeStruct((N, 2, 2, 2, 16, CH_...]
    reshape x2 -> x1, local copies, waits for them, and re-layouts: 6.8 us -> 3.41 us  [body(): xv = voltages.reshape(2, stations_here, 2, FRAMES_OWN, CH_LO, CH_HI)]
where the time goes in v1:
time: 113 us
  Pallas kernels  108 us (96%)
  local copies, waits for them, and re-layouts  4.68 us (4%)
    pallas_call x1, Pallas kernels, body(): pl.pallas_call(fused, out_shape=jax.ShapeDtypeStruct((N, 2, 2, 2, 16, CH_...  108 us
    reshape x1, local copies, waits for them, and re-layouts, body(): xv = voltages.reshape(2, stations_here, 2, FRAMES_OWN, CH_LO, CH_HI)  3.41 us

profile of v1, /device:TPU:64, one launch (start us, length us, event | category | flops | bytes accessed | tf_op | source)
XLA Modules:
  0.0 112.7 jit_solution(13689948296318165283)
XLA Ops:
  0.0 0.0 copy-start
  0.0 0.0 copy-start.1
  0.0 0.0 copy-start.2
  0.0 0.0 copy-start.3
  0.0 0.0 copy-start.4
  0.0 0.0 copy-start.5
  0.0 0.0 copy-start.6
  0.1 3.4 %reshape.12.xv = bf16[2,8,2,8,32,128]{5,4,3,2,1,0:T(8,128)(2,1)S(1)} reshape(bf16[2,8,2,32768]{3,2,1,0:T(2,128)(2,1)} %param.8) | data formatting | bytes 4194304 | tf_op jit(solution)/shard_map/reshape | solution.py:331
  3.5 0.0 copy-done
  3.5 0.0 copy-done.1
  3.5 0.0 copy-done.2
  3.5 0.0 copy-done.3
  3.5 0.0 copy-done.4
  3.5 0.0 copy-done.5
  3.5 0.0 copy-done.6
  3.5 107.9 %channelize_and_beamform.1 = bf16[16,2,2,2,16,128]{5,4,3,2,1,0:T(8,128)(2,1)S(1)} custom-call(s32[32]{0:T(128)S(1)} %copy-done.5, bf16[2,8,2,8,32,128]{5,4,3,2,1,0:T(8,128)(2,1)S(1)} %reshape.12.xv, f32[16,32,128]{2,1,0:T(8,128)S(1)} %copy-done.1, bf16[512,512]{1,0:T(8,128)(2,1)S(1)} %copy-done, bf16[256,256]{1,0:T(8,128)(2,1)S(1)} %copy-done.2, ...), custom_call_target="tpu_custom_call" | custom-call | tf_op jit(solution)/shard_map/channelize_and_beamform/pallas_call | solution.py:335
  111.4 1.2 %copy.9 = bf16[2,2,2,8,16,2,128]{6,5,4,3,2,1,0:T(2,128)(2,1)} copy(bf16[2,2,2,8,16,2,128]{6,4,5,1,0,2,3:T(8,128)(2,1)S(1)} %bitcast.5) | data formatting | bytes 1048576 | tf_op jit(solution)/shard_map/transpose | solution.py:368
Async XLA Ops:
  0.0 3.5 %copy-start = (bf16[512,512]{1,0:T(8,128)(2,1)S(1)}, bf16[512,512]{1,0:T(8,128)(2,1)}, u32[]{:S(2)}) copy-start(bf16[512,512]{1,0:T(8,128)(2,1)} %constant.13.low) | copy-start | bytes 1572868
  0.0 3.5 %copy-start.1 = (f32[16,32,128]{2,1,0:T(8,128)S(1)}, f32[16,32,128]{2,1,0:T(8,128)}, u32[]{:S(2)}) copy-start(f32[16,32,128]{2,1,0:T(8,128)} %constant.8.clone.win) | copy-start | bytes 786436
  0.0 3.5 %copy-start.2 = (bf16[256,256]{1,0:T(8,128)(2,1)S(1)}, bf16[256,256]{1,0:T(8,128)(2,1)}, u32[]{:S(2)}) copy-start(bf16[256,256]{1,0:T(8,128)(2,1)} %constant.14.high) | copy-start | bytes 393220
  0.0 3.5 %copy-start.3 = (f32[128,128]{1,0:T(8,128)S(1)}, f32[128,128]{1,0:T(8,128)}, u32[]{:S(2)}) copy-start(f32[128,128]{1,0:T(8,128)} %table.1) | copy-start | bytes 196612
  0.0 3.5 %copy-start.4 = (f32[32,2,256]{2,1,0:T(2,128)S(1)}, f32[32,2,256]{2,1,0:T(2,128)}, u32[]{:S(2)}) copy-start(f32[32,2,256]{2,1,0:T(2,128)} %constant.11.clone.twid) | copy-start | bytes 196612
  0.0 3.5 %copy-start.5 = (s32[32]{0:T(128)S(1)}, s32[32]{0:T(128)}, u32[]{:S(2)}) copy-start(s32[32]{0:T(128)} %pointing.1) | copy-start | bytes 388
  0.0 3.5 %copy-start.6 = (s32[128]{0:T(128)S(1)}, s32[128]{0:T(128)}, u32[]{:S(2)}) copy-start(s32[128]{0:T(128)} %param.11) | copy-start | bytes 1540

commit v2 on v1

v2 whole, which is shorter than its diff:
```python
import math

import jax
import jax.numpy as jnp
import numpy as np
from jax import lax
from jax.experimental import pallas as pl
from jax.experimental.pallas import tpu as pltpu
from jax.sharding import PartitionSpec as P

TAPS = 16
CH_LO = 32
CH_HI = 128
POINTS = CH_LO * CH_HI
GROUPS = 4
TWO_PI = 2.0 * math.pi
BF = jnp.bfloat16
F32 = jnp.float32
MESH = pl.DeviceIdType.MESH

N = 16
FRAMES_OWN = 8
STEPS = 8
BB = 8


def filter_window():
    position = np.arange(TAPS * POINTS, dtype=np.float64)
    total = float(TAPS * POINTS)
    taper = 0.5 - 0.5 * np.cos(2.0 * np.pi / total * position)
    kernel = np.sinc((position - 0.5 * total) / POINTS) * taper
    return jnp.asarray(kernel.reshape(TAPS, CH_LO, CH_HI).astype(np.float32))


def dft_table(points):
    counter = np.arange(points)
    angles = 2.0 * np.pi / points * (counter[:, None] * counter[None, :] % points)
    cosine = np.cos(angles) / math.sqrt(points)
    sine = np.sin(angles) / math.sqrt(points)
    return np.stack([np.stack([cosine, sine]), np.stack([-sine, cosine])])


def low_matrix():
    table = dft_table(CH_LO)
    eye = np.eye(8)
    full = np.einsum("oqkn,fg->kofgqn", table, eye)
    return jnp.asarray(full.reshape(512, 512).astype(np.float32)).astype(BF)


def high_matrix():
    table = dft_table(CH_HI)
    return jnp.asarray(
        table.transpose(1, 2, 0, 3).reshape(256, 256).astype(np.float32)
    ).astype(BF)


def twiddle_table():
    angle = 2.0 * np.pi / POINTS * (np.arange(CH_LO)[:, None] * np.arange(CH_HI)[None, :])
    pair = np.stack([np.cos(angle), np.sin(angle)], axis=1)
    return jnp.asarray(np.concatenate([pair, pair], axis=-1).astype(np.float32))


def turn_parts(turns):
    t = (turns - jnp.round(turns)) * math.pi
    y = t * t
    s = t * (
        1.0
        + y
        * (
            -1.0 / 6
            + y
            * (
                1.0 / 120
                + y * (-1.0 / 5040 + y * (1.0 / 362880 + y * (-1.0 / 39916800 + y / 6227020800.0)))
            )
        )
    )
    c = 1.0 + y * (
        -0.5
        + y
        * (
            1.0 / 24
            + y
            * (
                -1.0 / 720
                + y * (1.0 / 40320 + y * (-1.0 / 3628800 + y * (1.0 / 479001600)))
            )
        )
    )
    return 1.0 - 2.0 * s * s, 2.0 * s * c


def turn_of(step):
    return lax.rem(2 + 3 * step, 4)


def fused(
    pointing, xv, win, low, high, twid, table, group,
    out,
    rbuf, filt, first, rotated, chan, recv, delay, weights, acc, csend,
    entered, send_a, recv_a, send_r, recv_r, send_b, recv_b, send_c, recv_c,
):
    i = lax.axis_index("stn")
    j = lax.axis_index("tf")
    z, xh = i // 2, lax.rem(i, 2)
    station, half = j // 2, lax.rem(j, 2)
    own_half = j // 8
    keeps = own_half == half

    barrier = pltpu.get_barrier_semaphore()

    def greet(step, carry):
        pl.semaphore_signal(
            barrier, inc=1, device_id=(i, lax.rem(j + step, N)), device_id_type=MESH
        )
        pl.semaphore_signal(
            barrier, inc=1, device_id=(lax.rem(i + step, N), j), device_id_type=MESH
        )
        return carry

    lax.fori_loop(1, N, greet, 0)
    pl.semaphore_wait(barrier, 2 * (N - 1))

    def send_voltages(p):
        block = pl.ds(16 + 8 * lax.rem(j, 8), 8)

        def send(step, carry):
            s_to = lax.rem(station + step, 8)
            j_to = 2 * s_to + own_half

            @pl.when(j_to == j)
            def _():
                pltpu.make_async_copy(xv.at[:, s_to, p], rbuf.at[p, :, block], recv_a.at[p]).start()

            @pl.when(j_to != j)
            def _():
                pltpu.make_async_remote_copy(
                    src_ref=xv.at[:, s_to, p],
                    dst_ref=rbuf.at[p, :, block],
                    send_sem=send_a.at[p],
                    recv_sem=recv_a.at[p],
                    device_id=(i, j_to),
                    device_id_type=MESH,
                ).start()

            return carry

        lax.fori_loop(0, 8, send, 0)

    def wait_voltages_sent(p):
        @pl.when(keeps)
        def _():
            part = rbuf.at[p, :, pl.ds(0, 56)]
            pltpu.make_async_copy(part, part, send_a.at[p]).wait()

        @pl.when(jnp.logical_not(keeps))
        def _():
            part = rbuf.at[p, :, pl.ds(0, 64)]
            pltpu.make_async_copy(part, part, send_a.at[p]).wait()

    def relay(p):
        return pltpu.make_async_remote_copy(
            src_ref=rbuf.at[p, :, pl.ds(64, 16)],
            dst_ref=rbuf.at[p, :, pl.ds(0, 16)],
            send_sem=send_r.at[p],
            recv_sem=recv_r.at[p],
            device_id=(i, j + 1),
            device_id_type=MESH,
        )

    def take_voltages(p):
        part = rbuf.at[p, :, pl.ds(16, 64)]
        pltpu.make_async_copy(part, part, recv_a.at[p]).wait()

        @pl.when(half == 0)
        def _():
            relay(p).start()

        @pl.when(half == 1)
        def _():
            part = rbuf.at[p, :, pl.ds(0, 16)]
            pltpu.make_async_copy(part, part, recv_r.at[p]).wait()

    send_voltages(0)

    def tell(step, carry):
        pl.semaphore_signal(
            entered, inc=1, device_id=(i, lax.rem(j + step, N)), device_id_type=MESH
        )
        return carry

    lax.fori_loop(1, N, tell, 0)

    @pl.when(half == 0)
    def _():
        rbuf[:, :, pl.ds(0, 16)] = jnp.zeros((2, 2, 16, CH_LO, CH_HI), BF)

    groups = group[...]
    for b in range(BB):
        row = jnp.zeros((1, CH_HI), F32)
        for g in range(GROUPS):
            row = jnp.where(groups == g, table[pl.ds(pointing[4 * b + g], 1), :], row)
        delay[pl.ds(b, 1), :] = row
    lane = lax.broadcasted_iota(jnp.int32, (8, CH_HI), 1)
    whose = jnp.broadcast_to(groups, (8, CH_HI))

    def make_weights(part, carry):
        for more in range(4):
            s = part * 4 + more
            here = lane == s
            column = jnp.sum(jnp.where(here, delay[...], 0.0), axis=1, keepdims=True)
            mine = jnp.sum(jnp.where(here, whose, 0), axis=1, keepdims=True)
            for k2 in range(2):
                channel = (2 * j + k2) + CH_LO * lane
                fraction = channel.astype(F32) * (1.0 / POINTS)
                cosine, sine = turn_parts(column * fraction)
                scale = math.sqrt(GROUPS / 128)
                cosine = (scale * cosine).astype(BF).astype(F32)
                sine = (-scale * sine).astype(BF).astype(F32)
                for g in range(GROUPS):
                    weights[s, k2, 0, pl.ds(8 * g, 8), :] = jnp.where(mine == g, cosine, 0.0)
                    weights[s, k2, 1, pl.ds(8 * g, 8), :] = jnp.where(mine == g, sine, 0.0)
        return carry

    lax.fori_loop(0, 32, make_weights, 0)
    wait_voltages_sent(0)
    send_voltages(1)
    pl.semaphore_wait(entered, N - 1)

    def block(p, step):
        at = 4 * p + step
        near = lax.rem(z + turn_of(step), 4)
        fb = 4 * half + near

        def filter_part(part, inner):
            q = part // 2
            row = pl.multiple_of((part % 2) * 16, 16)
            for g2 in range(2):
                base = near * 16 + g2 * 8
                sums = [None] * 8
                taps = [win[t, pl.ds(row, 16), :] for t in range(TAPS)]
                for k in range(1, 24):
                    x = rbuf[p, q, base + k, pl.ds(row, 16), :].astype(F32)
                    for f in range(8):
                        t = k - 1 - f
                        if 0 <= t < TAPS:
                            term = taps[t] * x
                            sums[f] = term if sums[f] is None else sums[f] + term
                for f in range(8):
                    to = pl.ds(pl.multiple_of(f * 64 + q * 32 + row, 16), 16)
                    filt[to, pl.ds(128 * g2, 128)] = sums[f].astype(BF)
            return inner

        lax.fori_loop(0, 4, filter_part, 0)

        first[...] = jnp.dot(low[...], filt[...], preferred_element_type=F32).reshape(32, 2, 8, 256)

        def turn(c, inner):
            part = pl.ds(c * 8, 8)
            real, imag = first[part, 0], first[part, 1]
            cosine, sine = twid[part, 0:1, :], twid[part, 1:2, :]
            re = real * cosine + imag * sine
            im = imag * cosine - real * sine
            for g2 in range(2):
                lanes = slice(128 * g2, 128 * g2 + 128)
                both = jnp.concatenate([re[:, :, lanes], im[:, :, lanes]], axis=2).reshape(64, 256)
                rotated[pl.ds(pl.multiple_of(256 * g2 + 64 * c, 64), 64), :] = both.astype(BF)
            return inner

        lax.fori_loop(0, 4, turn, 0)
        done = jnp.dot(rotated[...], high[...], preferred_element_type=F32)
        chan[at] = done.astype(BF).reshape(2 * N, 16, 256)

        def send(n, inner):
            j_to = lax.rem(j + n, N)
            for g2 in range(2):
                here = jnp.logical_and(2 * fb + g2 == i, j_to == j)
                source = chan.at[at, N * g2 + j_to]
                target = recv.at[p, 8 * i + station]

                @pl.when(here)
                def _():
                    pltpu.make_async_copy(source, target, recv_b.at[p, i]).start()

                @pl.when(jnp.logical_not(here))
                def _():
                    pltpu.make_async_remote_copy(
                        src_ref=source,
                        dst_ref=target,
                        send_sem=send_b.at[at],
                        recv_sem=recv_b.at[p, i],
                        device_id=(2 * fb + g2, j_to),
                        device_id_type=MESH,
                    ).start()

            return inner

        lax.fori_loop(0, N, send, 0)

    def blocks(n, carry):
        p = n // 4

        @pl.when(lax.rem(n, 4) == 0)
        def _():
            take_voltages(p)

        block(p, lax.rem(n, 4))
        return carry

    lax.fori_loop(0, 8, blocks, 0)

    def add_block(p, step, last):
        z_from = lax.rem(z - turn_of(step // 4) + 8, 4) + 4 * lax.rem(step // 2, 2)
        i_from = 2 * z_from + lax.rem(step, 2)
        s0 = 8 * i_from
        part = recv.at[p, pl.ds(s0, 8)]
        pltpu.make_async_copy(part, part, recv_b.at[p, i_from]).wait()

        def some(g, inner):
            sums = [[[acc[g, b, q, k2] for k2 in range(2)] for q in range(2)] for b in range(BB)]
            for s in range(8):
                value = recv[p, s0 + s].astype(F32)
                for k2 in range(2):
                    vr = value[8 * k2 : 8 * k2 + 8, :128]
                    vi = value[8 * k2 : 8 * k2 + 8, 128:]
                    for b in range(BB):
                        wr = weights[s0 + s, k2, 0, pl.ds(8 * g + b, 1), :]
                        wi = weights[s0 + s, k2, 1, pl.ds(8 * g + b, 1), :]
                        sums[b][0][k2] = sums[b][0][k2] + (wr * vr - wi * vi)
                        sums[b][1][k2] = sums[b][1][k2] + (wr * vi + wi * vr)
            for b in range(BB):
                for q in range(2):
                    if last:
                        both = jnp.concatenate(sums[b][q], axis=0).astype(BF)
                        csend[p, 2 * b + g // 2, lax.rem(g, 2), q] = both
                    else:
                        for k2 in range(2):
                            acc[g, b, q, k2] = sums[b][q][k2]
            return inner

        lax.fori_loop(0, GROUPS, some, 0)

    def beams(p, carry):
        acc[...] = jnp.zeros(acc.shape, F32)

        def add_early(step, inner):
            add_block(p, step, False)
            return inner

        lax.fori_loop(0, N - 1, add_early, 0)
        add_block(p, jnp.int32(N - 1), True)
        pltpu.make_async_copy(csend.at[p, i], out.at[p, i], recv_c.at[p]).start()

        def send_beams(step, inner):
            target = lax.rem(i + step, N)
            pltpu.make_async_remote_copy(
                src_ref=csend.at[p, target],
                dst_ref=out.at[p, i],
                send_sem=send_c.at[p],
                recv_sem=recv_c.at[p],
                device_id=(target, j),
                device_id_type=MESH,
            ).start()
            return inner

        lax.fori_loop(1, N, send_beams, 0)
        return carry

    lax.fori_loop(0, 2, beams, 0)

    wait_voltages_sent(1)

    @pl.when(half == 0)
    def _():
        for p in range(2):
            relay(p).wait_send()

    def wait_sent(at, carry):
        fb = 4 * half + lax.rem(z + turn_of(lax.rem(at, 4)), 4)
        mine = fb == z

        @pl.when(mine)
        def _():
            part = chan.at[at, pl.ds(0, 2 * N - 1)]
            pltpu.make_async_copy(part, part, send_b.at[at]).wait()

        @pl.when(jnp.logical_not(mine))
        def _():
            pltpu.make_async_copy(chan.at[at], chan.at[at], send_b.at[at]).wait()

        return carry

    lax.fori_loop(0, STEPS, wait_sent, 0)
    for p in range(2):
        part = csend.at[p, pl.ds(0, N - 1)]
        pltpu.make_async_copy(part, part, send_c.at[p]).wait()
        pltpu.make_async_copy(csend.at[p], csend.at[p], recv_c.at[p]).wait()


def body(voltages, delay_table, beam_pointing, station_group):
    stations_here = voltages.shape[1]
    xv = voltages.reshape(2, stations_here, 2, FRAMES_OWN, CH_LO, CH_HI)

    vmem = pl.BlockSpec(memory_space=pltpu.VMEM)
    anywhere = pl.BlockSpec(memory_space=pl.ANY)
    out = pl.pallas_call(
        fused,
        out_shape=jax.ShapeDtypeStruct((2, N, 2, 2, 16, CH_HI), BF),
        in_specs=[pl.BlockSpec(memory_space=pltpu.SMEM), anywhere] + [vmem] * 6,
        out_specs=anywhere,
        scratch_shapes=[
            pltpu.VMEM((2, 2, 80, CH_LO, CH_HI), BF),
            pltpu.VMEM((512, 256), BF),
            pltpu.VMEM((CH_LO, 2, 8, 256), F32),
            pltpu.VMEM((512, 256), BF),
            pltpu.VMEM((STEPS, 2 * N, 16, 256), BF),
            pltpu.VMEM((2, 128, 16, 256), BF),
            pltpu.VMEM((8, 128), F32),
            pltpu.VMEM((128, 2, 2, 32, CH_HI), F32),
            pltpu.VMEM((GROUPS, BB, 2, 2, 8, CH_HI), F32),
            pltpu.VMEM((2, N, 2, 2, 16, CH_HI), BF),
            pltpu.SemaphoreType.REGULAR,
            pltpu.SemaphoreType.DMA((2,)),
            pltpu.SemaphoreType.DMA((2,)),
            pltpu.SemaphoreType.DMA((2,)),
            pltpu.SemaphoreType.DMA((2,)),
            pltpu.SemaphoreType.DMA((STEPS,)),
            pltpu.SemaphoreType.DMA((2, N)),
            pltpu.SemaphoreType.DMA((2,)),
            pltpu.SemaphoreType.DMA((2,)),
        ],
        compiler_params=pltpu.CompilerParams(
            has_side_effects=True, collective_id=0, vmem_limit_bytes=40 * 1024 * 1024
        ),
        name="channelize_and_beamform",
    )(
        beam_pointing, xv, filter_window(), low_matrix(), high_matrix(), twiddle_table(),
        delay_table, station_group.reshape(1, -1),
    )

    out = out.reshape(2, N, 2, 2, 2, 8, CH_HI).transpose(2, 3, 0, 1, 5, 4, 6)
    return out.reshape(2, 2, 2, 128, 2, CH_HI)


def solution(mesh):
    in_specs = (P(None, "stn", None, "tf"), P(), P(), P())
    out_specs = P("stn", None, None, None, "tf", None)
    return jax.shard_map(body, mesh=mesh, in_specs=in_specs, out_specs=out_specs, check_vma=False)
```

time: 113 us -> 101 us (0.89)
  Pallas kernels: 108 us -> 96.3 us
    pallas_call x1, Pallas kernels: 108 us -> 96.3 us  [body(): pl.pallas_call(fused, out_shape=jax.ShapeDtypeStruct((2, N, 2, 2, 16, CH_...]
where the time goes in v2:
time: 101 us
  Pallas kernels  96.3 us (95%)
  local copies, waits for them, and re-layouts  4.66 us (5%)
    pallas_call x1, Pallas kernels, body(): pl.pallas_call(fused, out_shape=jax.ShapeDtypeStruct((2, N, 2, 2, 16, CH_...  96.3 us
    reshape x1, local copies, waits for them, and re-layouts, body(): xv = voltages.reshape(2, stations_here, 2, FRAMES_OWN, CH_LO, CH_HI)  3.41 us

profile of v2, /device:TPU:64, one launch (start us, length us, event | category | flops | bytes accessed | tf_op | source)
XLA Modules:
  0.0 101.0 jit_solution(4605473859544701318)
XLA Ops:
  0.0 0.0 copy-start
  0.0 0.0 copy-start.1
  0.0 0.0 copy-start.2
  0.0 0.0 copy-start.3
  0.0 0.0 copy-start.4
  0.0 0.0 copy-start.5
  0.0 0.0 copy-start.6
  0.1 3.4 %reshape.12.xv = bf16[2,8,2,8,32,128]{5,4,3,2,1,0:T(8,128)(2,1)S(1)} reshape(bf16[2,8,2,32768]{3,2,1,0:T(2,128)(2,1)} %param.8) | data formatting | bytes 4194304 | tf_op jit(solution)/shard_map/reshape | solution.py:402
  3.5 0.0 copy-done
  3.5 0.0 copy-done.1
  3.5 0.0 copy-done.2
  3.5 0.0 copy-done.3
  3.5 0.0 copy-done.4
  3.5 0.0 copy-done.5
  3.5 0.0 copy-done.6
  3.5 96.3 %channelize_and_beamform.1 = bf16[2,16,2,2,16,128]{5,4,3,2,1,0:T(8,128)(2,1)S(1)} custom-call(s32[32]{0:T(128)S(1)} %copy-done.5, bf16[2,8,2,8,32,128]{5,4,3,2,1,0:T(8,128)(2,1)S(1)} %reshape.12.xv, f32[16,32,128]{2,1,0:T(8,128)S(1)} %copy-done.1, bf16[512,512]{1,0:T(8,128)(2,1)S(1)} %copy-done, bf16[256,256]{1,0:T(8,128)(2,1)S(1)} %copy-done.2, ...), custom_call_target="tpu_custom_call" | custom-call | tf_op jit(solution)/shard_map/channelize_and_beamform/pallas_call | solution.py:406
  99.8 1.2 %copy.9 = bf16[2,2,2,16,8,2,128]{6,5,4,3,2,1,0:T(2,128)(2,1)} copy(bf16[2,2,2,16,8,2,128]{6,4,5,1,0,3,2:T(8,128)(2,1)S(1)} %bitcast.5) | data formatting | bytes 1048576 | tf_op jit(solution)/shard_map/transpose | solution.py:441
Async XLA Ops:
  0.0 3.5 %copy-start = (bf16[512,512]{1,0:T(8,128)(2,1)S(1)}, bf16[512,512]{1,0:T(8,128)(2,1)}, u32[]{:S(2)}) copy-start(bf16[512,512]{1,0:T(8,128)(2,1)} %constant.13.low) | copy-start | bytes 1572868
  0.0 3.5 %copy-start.1 = (f32[16,32,128]{2,1,0:T(8,128)S(1)}, f32[16,32,128]{2,1,0:T(8,128)}, u32[]{:S(2)}) copy-start(f32[16,32,128]{2,1,0:T(8,128)} %constant.8.clone.win) | copy-start | bytes 786436
  0.0 3.5 %copy-start.2 = (bf16[256,256]{1,0:T(8,128)(2,1)S(1)}, bf16[256,256]{1,0:T(8,128)(2,1)}, u32[]{:S(2)}) copy-start(bf16[256,256]{1,0:T(8,128)(2,1)} %constant.14.high) | copy-start | bytes 393220
  0.0 3.5 %copy-start.3 = (f32[128,128]{1,0:T(8,128)S(1)}, f32[128,128]{1,0:T(8,128)}, u32[]{:S(2)}) copy-start(f32[128,128]{1,0:T(8,128)} %table.1) | copy-start | bytes 196612
  0.0 3.5 %copy-start.4 = (f32[32,2,256]{2,1,0:T(2,128)S(1)}, f32[32,2,256]{2,1,0:T(2,128)}, u32[]{:S(2)}) copy-start(f32[32,2,256]{2,1,0:T(2,128)} %constant.11.clone.twid) | copy-start | bytes 196612
  0.0 3.5 %copy-start.5 = (s32[32]{0:T(128)S(1)}, s32[32]{0:T(128)}, u32[]{:S(2)}) copy-start(s32[32]{0:T(128)} %pointing.1) | copy-start | bytes 388
  0.0 3.5 %copy-start.6 = (s32[128]{0:T(128)S(1)}, s32[128]{0:T(128)}, u32[]{:S(2)}) copy-start(s32[128]{0:T(128)} %param.11) | copy-start | bytes 1540

commit v3 on v2

--- a/solution.py
+++ b/solution.py
@@ -97,12 +97,13 @@
 def fused(
     pointing, xv, win, low, high, twid, table, group,
     out,
-    rbuf, filt, first, rotated, chan, recv, delay, weights, acc, csend,
-    entered, send_a, recv_a, send_r, recv_r, send_b, recv_b, send_c, recv_c,
+    rbuf, filt, first, rotated, chan, recv_0, recv_1, delay, weights, order, running, csend,
+    order_smem, order_sem, entered, send_a, recv_a, send_r, recv_r, send_b, recv_b, send_c, recv_c,
 ):
     i = lax.axis_index("stn")
     j = lax.axis_index("tf")
-    z, xh = i // 2, lax.rem(i, 2)
+    z = i // 2
+    recv = (recv_0, recv_1)
     station, half = j // 2, lax.rem(j, 2)
     own_half = j // 8
     keeps = own_half == half
@@ -176,11 +177,6 @@
         def _():
             relay(p).start()
 
-        @pl.when(half == 1)
-        def _():
-            part = rbuf.at[p, :, pl.ds(0, 16)]
-            pltpu.make_async_copy(part, part, recv_r.at[p]).wait()
-
     send_voltages(0)
 
     def tell(step, carry):
@@ -202,27 +198,41 @@
             row = jnp.where(groups == g, table[pl.ds(pointing[4 * b + g], 1), :], row)
         delay[pl.ds(b, 1), :] = row
     lane = lax.broadcasted_iota(jnp.int32, (8, CH_HI), 1)
-    whose = jnp.broadcast_to(groups, (8, CH_HI))
+
+    wide = jnp.broadcast_to(groups, (128, CH_HI))
+    lanes = lax.broadcasted_iota(jnp.int32, (128, CH_HI), 1)
+    rows = lax.broadcasted_iota(jnp.int32, (128, CH_HI), 0)
+    own = jnp.sum(jnp.where(rows == lanes, wide, 0), axis=1, keepdims=True)
+    ahead = jnp.logical_or(wide < own, jnp.logical_and(wide == own, lanes < rows))
+    place = jnp.sum(jnp.where(ahead, 1, 0), axis=1, keepdims=True)
+    starts = jnp.sum(jnp.where(own < lanes, 1, 0), axis=0, keepdims=True)
+    opens = jnp.zeros((1, CH_HI), jnp.int32)
+    for g in range(GROUPS):
+        opens = jnp.where(starts[:, g : g + 1] == lanes[:1], 1, opens)
+    order[...] = jnp.zeros((8, CH_HI), jnp.int32)
+    order[pl.ds(0, 1), :] = jnp.sum(jnp.where(place == lanes, rows, 0), axis=0, keepdims=True)
+    order[pl.ds(1, 1), :] = opens
+    order[pl.ds(2, 1), :] = starts
+    order[pl.ds(3, 1), :] = jnp.sum(jnp.where(own <= lanes, 1, 0), axis=0, keepdims=True)
+    order_copy = pltpu.make_async_copy(order, order_smem, order_sem)
+    order_copy.start()
 
     def make_weights(part, carry):
         for more in range(4):
             s = part * 4 + more
             here = lane == s
             column = jnp.sum(jnp.where(here, delay[...], 0.0), axis=1, keepdims=True)
-            mine = jnp.sum(jnp.where(here, whose, 0), axis=1, keepdims=True)
             for k2 in range(2):
                 channel = (2 * j + k2) + CH_LO * lane
                 fraction = channel.astype(F32) * (1.0 / POINTS)
                 cosine, sine = turn_parts(column * fraction)
                 scale = math.sqrt(GROUPS / 128)
-                cosine = (scale * cosine).astype(BF).astype(F32)
-                sine = (-scale * sine).astype(BF).astype(F32)
-                for g in range(GROUPS):
-                    weights[s, k2, 0, pl.ds(8 * g, 8), :] = jnp.where(mine == g, cosine, 0.0)
-                    weights[s, k2, 1, pl.ds(8 * g, 8), :] = jnp.where(mine == g, sine, 0.0)
+                weights[s, k2, 0] = (scale * cosine).astype(BF).astype(F32)
+                weights[s, k2, 1] = (-scale * sine).astype(BF).astype(F32)
         return carry
 
     lax.fori_loop(0, 32, make_weights, 0)
+    order_copy.wait()
     wait_voltages_sent(0)
     send_voltages(1)
     pl.semaphore_wait(entered, N - 1)
@@ -230,6 +240,12 @@
     def block(p, step):
         at = 4 * p + step
         near = lax.rem(z + turn_of(step), 4)
+
+        @pl.when(jnp.logical_and(half == 1, near == 0))
+        def _():
+            part = rbuf.at[p, :, pl.ds(0, 16)]
+            pltpu.make_async_copy(part, part, recv_r.at[p]).wait()
+
         fb = 4 * half + near
 
         def filter_part(part, inner):
@@ -276,7 +292,7 @@
             for g2 in range(2):
                 here = jnp.logical_and(2 * fb + g2 == i, j_to == j)
                 source = chan.at[at, N * g2 + j_to]
-                target = recv.at[p, 8 * i + station]
+                target = recv[p].at[8 * i + station]
 
                 @pl.when(here)
                 def _():
@@ -297,58 +313,62 @@
 
         lax.fori_loop(0, N, send, 0)
 
-    def blocks(n, carry):
-        p = n // 4
-
-        @pl.when(lax.rem(n, 4) == 0)
-        def _():
-            take_voltages(p)
-
-        block(p, lax.rem(n, 4))
-        return carry
-
-    lax.fori_loop(0, 8, blocks, 0)
-
-    def add_block(p, step, last):
-        z_from = lax.rem(z - turn_of(step // 4) + 8, 4) + 4 * lax.rem(step // 2, 2)
-        i_from = 2 * z_from + lax.rem(step, 2)
-        s0 = 8 * i_from
-        part = recv.at[p, pl.ds(s0, 8)]
-        pltpu.make_async_copy(part, part, recv_b.at[p, i_from]).wait()
-
-        def some(g, inner):
-            sums = [[[acc[g, b, q, k2] for k2 in range(2)] for q in range(2)] for b in range(BB)]
-            for s in range(8):
-                value = recv[p, s0 + s].astype(F32)
-                for k2 in range(2):
-                    vr = value[8 * k2 : 8 * k2 + 8, :128]
-                    vi = value[8 * k2 : 8 * k2 + 8, 128:]
-                    for b in range(BB):
-                        wr = weights[s0 + s, k2, 0, pl.ds(8 * g + b, 1), :]
-                        wi = weights[s0 + s, k2, 1, pl.ds(8 * g + b, 1), :]
-                        sums[b][0][k2] = sums[b][0][k2] + (wr * vr - wi * vi)
-                        sums[b][1][k2] = sums[b][1][k2] + (wr * vi + wi * vr)
+    for p in range(2):
+        take_voltages(p)
+
+        def blocks(step, carry, p=p):
+            block(p, step)
+            return carry
+
+        lax.fori_loop(0, 4, blocks, 0)
+
+    def beams(p):
+        def arrive(i_from, carry):
+            part = recv[p].at[pl.ds(8 * i_from, 8)]
+            pltpu.make_async_copy(part, part, recv_b.at[p, i_from]).wait()
+            return carry
+
+        lax.fori_loop(0, N, arrive, 0)
+
+        def add(m, sums):
+            s = order_smem[0, m]
+            keep = jnp.where(order_smem[1, m] > 0, 0.0, 1.0)
+            value = recv[p][s].astype(F32)
+            result = []
+            for k2 in range(2):
+                vr = value[8 * k2 : 8 * k2 + 8, :128]
+                vi = value[8 * k2 : 8 * k2 + 8, 128:]
+                for b in range(BB):
+                    wr = weights[s, k2, 0, pl.ds(b, 1), :]
+                    wi = weights[s, k2, 1, pl.ds(b, 1), :]
+                    re, im = sums[2 * (BB * k2 + b)], sums[2 * (BB * k2 + b) + 1]
+                    re = keep * re + (wr * vr - wi * vi)
+                    im = keep * im + (wr * vi + wi * vr)
+                    running[m, b, 0, k2] = re
+                    running[m, b, 1, k2] = im
+                    result += [re, im]
+            return tuple(result)
+
+        zero = jnp.zeros((8, CH_HI), F32)
+
+        def add_some(part, sums):
+            for more in range(2):
+                sums = add(part * 2 + more, sums)
+            return sums
+
+        lax.fori_loop(0, 128 // 2, add_some, (zero,) * (4 * BB))
+
+        def finish(g, carry):
+            start, stop = order_smem[2, g], order_smem[3, g]
+            some = jnp.where(stop > start, 1.0, 0.0)
+            at = jnp.maximum(stop - 1, 0)
             for b in range(BB):
                 for q in range(2):
-                    if last:
-                        both = jnp.concatenate(sums[b][q], axis=0).astype(BF)
-                        csend[p, 2 * b + g // 2, lax.rem(g, 2), q] = both
-                    else:
-                        for k2 in range(2):
-                            acc[g, b, q, k2] = sums[b][q][k2]
-            return inner
-
-        lax.fori_loop(0, GROUPS, some, 0)
-
-    def beams(p, carry):
-        acc[...] = jnp.zeros(acc.shape, F32)
-
-        def add_early(step, inner):
-            add_block(p, step, False)
-            return inner
-
-        lax.fori_loop(0, N - 1, add_early, 0)
-        add_block(p, jnp.int32(N - 1), True)
+                    total = some * running[at, b, q].reshape(16, CH_HI)
+                    csend[p, 2 * b + g // 2, lax.rem(g, 2), q] = total.astype(BF)
+            return carry
+
+        lax.fori_loop(0, GROUPS, finish, 0)
         pltpu.make_async_copy(csend.at[p, i], out.at[p, i], recv_c.at[p]).start()
 
         def send_beams(step, inner):
@@ -364,9 +384,9 @@
             return inner
 
         lax.fori_loop(1, N, send_beams, 0)
-        return carry
-
-    lax.fori_loop(0, 2, beams, 0)
+
+    for p in range(2):
+        beams(p)
 
     wait_voltages_sent(1)
 
@@ -414,11 +434,15 @@
             pltpu.VMEM((CH_LO, 2, 8, 256), F32),
             pltpu.VMEM((512, 256), BF),
             pltpu.VMEM((STEPS, 2 * N, 16, 256), BF),
-            pltpu.VMEM((2, 128, 16, 256), BF),
+            pltpu.VMEM((128, 16, 256), BF),
+            pltpu.VMEM((128, 16, 256), BF),
             pltpu.VMEM((8, 128), F32),
-            pltpu.VMEM((128, 2, 2, 32, CH_HI), F32),
-            pltpu.VMEM((GROUPS, BB, 2, 2, 8, CH_HI), F32),
+            pltpu.VMEM((128, 2, 2, BB, CH_HI), F32),
+            pltpu.VMEM((8, CH_HI), jnp.int32),
+            pltpu.VMEM((128, BB, 2, 2, 8, CH_HI), F32),
             pltpu.VMEM((2, N, 2, 2, 16, CH_HI), BF),
+            pltpu.SMEM((8, CH_HI), jnp.int32),
+            pltpu.SemaphoreType.DMA,
             pltpu.SemaphoreType.REGULAR,
             pltpu.SemaphoreType.DMA((2,)),
             pltpu.SemaphoreType.DMA((2,)),

time: 101 us -> 98.8 us (0.978)
  Pallas kernels: 96.3 us -> 93.4 us
    pallas_call x1, Pallas kernels: 96.3 us -> 93.4 us  [body(): pl.pallas_call(fused, out_shape=jax.ShapeDtypeStruct((2, N, 2, 2, 16, CH_...]
where the time goes in v3:
time: 98.8 us; the launch traced here: 98.1 us
  Pallas kernels  93.4 us (95%)
  local copies, waits for them, and re-layouts  4.66 us (5%)
    pallas_call x1, Pallas kernels, body(): pl.pallas_call(fused, out_shape=jax.ShapeDtypeStruct((2, N, 2, 2, 16, CH_...  93.4 us
    reshape x1, local copies, waits for them, and re-layouts, body(): xv = voltages.reshape(2, stations_here, 2, FRAMES_OWN, CH_LO, CH_HI)  3.41 us

profile of v3, /device:TPU:64, one launch (start us, length us, event | category | flops | bytes accessed | tf_op | source)
XLA Modules:
  0.0 98.1 jit_solution(12633144576769472255)
XLA Ops:
  0.0 0.0 copy-start
  0.0 0.0 copy-start.1
  0.0 0.0 copy-start.2
  0.0 0.0 copy-start.3
  0.0 0.0 copy-start.4
  0.0 0.0 copy-start.5
  0.0 0.0 copy-start.6
  0.1 3.4 %reshape.12.xv = bf16[2,8,2,8,32,128]{5,4,3,2,1,0:T(8,128)(2,1)S(1)} reshape(bf16[2,8,2,32768]{3,2,1,0:T(2,128)(2,1)} %param.8) | data formatting | bytes 4194304 | tf_op jit(solution)/shard_map/reshape | solution.py:422
  3.5 0.0 copy-done
  3.5 0.0 copy-done.1
  3.5 0.0 copy-done.2
  3.5 0.0 copy-done.3
  3.5 0.0 copy-done.4
  3.5 0.0 copy-done.5
  3.5 0.0 copy-done.6
  3.5 93.4 %channelize_and_beamform.1 = bf16[2,16,2,2,16,128]{5,4,3,2,1,0:T(8,128)(2,1)S(1)} custom-call(s32[32]{0:T(128)S(1)} %copy-done.5, bf16[2,8,2,8,32,128]{5,4,3,2,1,0:T(8,128)(2,1)S(1)} %reshape.12.xv, f32[16,32,128]{2,1,0:T(8,128)S(1)} %copy-done.1, bf16[512,512]{1,0:T(8,128)(2,1)S(1)} %copy-done, bf16[256,256]{1,0:T(8,128)(2,1)S(1)} %copy-done.2, ...), custom_call_target="tpu_custom_call" | custom-call | tf_op jit(solution)/shard_map/channelize_and_beamform/pallas_call | solution.py:426
  96.9 1.2 %copy.9 = bf16[2,2,2,16,8,2,128]{6,5,4,3,2,1,0:T(2,128)(2,1)} copy(bf16[2,2,2,16,8,2,128]{6,4,5,1,0,3,2:T(8,128)(2,1)S(1)} %bitcast.5) | data formatting | bytes 1048576 | tf_op jit(solution)/shard_map/transpose | solution.py:465
Async XLA Ops:
  0.0 3.5 %copy-start = (bf16[512,512]{1,0:T(8,128)(2,1)S(1)}, bf16[512,512]{1,0:T(8,128)(2,1)}, u32[]{:S(2)}) copy-start(bf16[512,512]{1,0:T(8,128)(2,1)} %constant.13.low) | copy-start | bytes 1572868
  0.0 3.5 %copy-start.1 = (f32[16,32,128]{2,1,0:T(8,128)S(1)}, f32[16,32,128]{2,1,0:T(8,128)}, u32[]{:S(2)}) copy-start(f32[16,32,128]{2,1,0:T(8,128)} %constant.8.clone.win) | copy-start | bytes 786436
  0.0 3.5 %copy-start.2 = (bf16[256,256]{1,0:T(8,128)(2,1)S(1)}, bf16[256,256]{1,0:T(8,128)(2,1)}, u32[]{:S(2)}) copy-start(bf16[256,256]{1,0:T(8,128)(2,1)} %constant.14.high) | copy-start | bytes 393220
  0.0 3.5 %copy-start.3 = (f32[128,128]{1,0:T(8,128)S(1)}, f32[128,128]{1,0:T(8,128)}, u32[]{:S(2)}) copy-start(f32[128,128]{1,0:T(8,128)} %table.1) | copy-start | bytes 196612
  0.0 3.5 %copy-start.4 = (f32[32,2,256]{2,1,0:T(2,128)S(1)}, f32[32,2,256]{2,1,0:T(2,128)}, u32[]{:S(2)}) copy-start(f32[32,2,256]{2,1,0:T(2,128)} %constant.11.clone.twid) | copy-start | bytes 196612
  0.0 3.5 %copy-start.5 = (s32[32]{0:T(128)S(1)}, s32[32]{0:T(128)}, u32[]{:S(2)}) copy-start(s32[32]{0:T(128)} %pointing.1) | copy-start | bytes 388
  0.0 3.5 %copy-start.6 = (s32[128]{0:T(128)S(1)}, s32[128]{0:T(128)}, u32[]{:S(2)}) copy-start(s32[128]{0:T(128)} %param.11) | copy-start | bytes 1540

commit v4 on v3

--- a/solution.py
+++ b/solution.py
@@ -91,7 +91,7 @@
 
 
 def turn_of(step):
-    return lax.rem(2 + 3 * step, 4)
+    return lax.rem(step, 4)
 
 
 def fused(

time: 98.8 us -> 96.2 us (0.974)
  Pallas kernels: 93.4 us -> 91.2 us
    pallas_call x1, Pallas kernels: 93.4 us -> 91.2 us  [body(): pl.pallas_call(fused, out_shape=jax.ShapeDtypeStruct((2, N, 2, 2, 16, CH_...]
where the time goes in v4:
time: 96.2 us; the launch traced here: 95.9 us
  Pallas kernels  91.2 us (95%)
  local copies, waits for them, and re-layouts  4.66 us (5%)
    pallas_call x1, Pallas kernels, body(): pl.pallas_call(fused, out_shape=jax.ShapeDtypeStruct((2, N, 2, 2, 16, CH_...  91.2 us
    reshape x1, local copies, waits for them, and re-layouts, body(): xv = voltages.reshape(2, stations_here, 2, FRAMES_OWN, CH_LO, CH_HI)  3.41 us

profile of v4, /device:TPU:64, one launch (start us, length us, event | category | flops | bytes accessed | tf_op | source)
XLA Modules:
  0.0 95.9 jit_solution(14125271233072783393)
XLA Ops:
  0.0 0.0 copy-start
  0.0 0.0 copy-start.1
  0.0 0.0 copy-start.2
  0.0 0.0 copy-start.3
  0.0 0.0 copy-start.4
  0.0 0.0 copy-start.5
  0.0 0.0 copy-start.6
  0.1 3.4 %reshape.12.xv = bf16[2,8,2,8,32,128]{5,4,3,2,1,0:T(8,128)(2,1)S(1)} reshape(bf16[2,8,2,32768]{3,2,1,0:T(2,128)(2,1)} %param.8) | data formatting | bytes 4194304 | tf_op jit(solution)/shard_map/reshape | solution.py:422
  3.5 0.0 copy-done
  3.5 0.0 copy-done.1
  3.5 0.0 copy-done.2
  3.5 0.0 copy-done.3
  3.5 0.0 copy-done.4
  3.5 0.0 copy-done.5
  3.5 0.0 copy-done.6
  3.5 91.2 %channelize_and_beamform.1 = bf16[2,16,2,2,16,128]{5,4,3,2,1,0:T(8,128)(2,1)S(1)} custom-call(s32[32]{0:T(128)S(1)} %copy-done.5, bf16[2,8,2,8,32,128]{5,4,3,2,1,0:T(8,128)(2,1)S(1)} %reshape.12.xv, f32[16,32,128]{2,1,0:T(8,128)S(1)} %copy-done.1, bf16[512,512]{1,0:T(8,128)(2,1)S(1)} %copy-done, bf16[256,256]{1,0:T(8,128)(2,1)S(1)} %copy-done.2, ...), custom_call_target="tpu_custom_call" | custom-call | tf_op jit(solution)/shard_map/channelize_and_beamform/pallas_call | solution.py:426
  94.7 1.2 %copy.9 = bf16[2,2,2,16,8,2,128]{6,5,4,3,2,1,0:T(2,128)(2,1)} copy(bf16[2,2,2,16,8,2,128]{6,4,5,1,0,3,2:T(8,128)(2,1)S(1)} %bitcast.5) | data formatting | bytes 1048576 | tf_op jit(solution)/shard_map/transpose | solution.py:465
Async XLA Ops:
  0.0 3.5 %copy-start = (bf16[512,512]{1,0:T(8,128)(2,1)S(1)}, bf16[512,512]{1,0:T(8,128)(2,1)}, u32[]{:S(2)}) copy-start(bf16[512,512]{1,0:T(8,128)(2,1)} %constant.13.low) | copy-start | bytes 1572868
  0.0 3.5 %copy-start.1 = (f32[16,32,128]{2,1,0:T(8,128)S(1)}, f32[16,32,128]{2,1,0:T(8,128)}, u32[]{:S(2)}) copy-start(f32[16,32,128]{2,1,0:T(8,128)} %constant.8.clone.win) | copy-start | bytes 786436
  0.0 3.5 %copy-start.2 = (bf16[256,256]{1,0:T(8,128)(2,1)S(1)}, bf16[256,256]{1,0:T(8,128)(2,1)}, u32[]{:S(2)}) copy-start(bf16[256,256]{1,0:T(8,128)(2,1)} %constant.14.high) | copy-start | bytes 393220
  0.0 3.5 %copy-start.3 = (f32[128,128]{1,0:T(8,128)S(1)}, f32[128,128]{1,0:T(8,128)}, u32[]{:S(2)}) copy-start(f32[128,128]{1,0:T(8,128)} %table.1) | copy-start | bytes 196612
  0.0 3.5 %copy-start.4 = (f32[32,2,256]{2,1,0:T(2,128)S(1)}, f32[32,2,256]{2,1,0:T(2,128)}, u32[]{:S(2)}) copy-start(f32[32,2,256]{2,1,0:T(2,128)} %constant.11.clone.twid) | copy-start | bytes 196612
  0.0 3.5 %copy-start.5 = (s32[32]{0:T(128)S(1)}, s32[32]{0:T(128)}, u32[]{:S(2)}) copy-start(s32[32]{0:T(128)} %pointing.1) | copy-start | bytes 388
  0.0 3.5 %copy-start.6 = (s32[128]{0:T(128)S(1)}, s32[128]{0:T(128)}, u32[]{:S(2)}) copy-start(s32[128]{0:T(128)} %param.11) | copy-start | bytes 1540

commit v5 on v4

--- a/solution.py
+++ b/solution.py
@@ -352,11 +352,11 @@
         zero = jnp.zeros((8, CH_HI), F32)
 
         def add_some(part, sums):
-            for more in range(2):
-                sums = add(part * 2 + more, sums)
+            for more in range(4):
+                sums = add(part * 4 + more, sums)
             return sums
 
-        lax.fori_loop(0, 128 // 2, add_some, (zero,) * (4 * BB))
+        lax.fori_loop(0, 128 // 4, add_some, (zero,) * (4 * BB))
 
         def finish(g, carry):
             start, stop = order_smem[2, g], order_smem[3, g]

time: 96.2 us -> 96.9 us (level); the launches traced: 95.9 us -> 95.6 us
  no operation moved by 1% of the time
where the time goes in v5:
time: 96.9 us; the launch traced here: 95.6 us
  Pallas kernels  90.8 us (94%)
  local copies, waits for them, and re-layouts  4.66 us (5%)
    pallas_call x1, Pallas kernels, body(): pl.pallas_call(fused, out_shape=jax.ShapeDtypeStruct((2, N, 2, 2, 16, CH_...  90.8 us
    reshape x1, local copies, waits for them, and re-layouts, body(): xv = voltages.reshape(2, stations_here, 2, FRAMES_OWN, CH_LO, CH_HI)  3.41 us

profile of v5, /device:TPU:64, one launch (start us, length us, event | category | flops | bytes accessed | tf_op | source)
XLA Modules:
  0.0 95.6 jit_solution(4006961381825627098)
XLA Ops:
  0.0 0.0 copy-start
  0.0 0.0 copy-start.1
  0.0 0.0 copy-start.2
  0.0 0.0 copy-start.3
  0.0 0.0 copy-start.4
  0.0 0.0 copy-start.5
  0.0 0.0 copy-start.6
  0.1 3.4 %reshape.12.xv = bf16[2,8,2,8,32,128]{5,4,3,2,1,0:T(8,128)(2,1)S(1)} reshape(bf16[2,8,2,32768]{3,2,1,0:T(2,128)(2,1)} %param.8) | data formatting | bytes 4194304 | tf_op jit(solution)/shard_map/reshape | solution.py:422
  3.5 0.0 copy-done
  3.5 0.0 copy-done.1
  3.5 0.0 copy-done.2
  3.5 0.0 copy-done.3
  3.5 0.0 copy-done.4
  3.5 0.0 copy-done.5
  3.5 0.0 copy-done.6
  3.5 90.8 %channelize_and_beamform.1 = bf16[2,16,2,2,16,128]{5,4,3,2,1,0:T(8,128)(2,1)S(1)} custom-call(s32[32]{0:T(128)S(1)} %copy-done.5, bf16[2,8,2,8,32,128]{5,4,3,2,1,0:T(8,128)(2,1)S(1)} %reshape.12.xv, f32[16,32,128]{2,1,0:T(8,128)S(1)} %copy-done.1, bf16[512,512]{1,0:T(8,128)(2,1)S(1)} %copy-done, bf16[256,256]{1,0:T(8,128)(2,1)S(1)} %copy-done.2, ...), custom_call_target="tpu_custom_call" | custom-call | tf_op jit(solution)/shard_map/channelize_and_beamform/pallas_call | solution.py:426
  94.4 1.2 %copy.9 = bf16[2,2,2,16,8,2,128]{6,5,4,3,2,1,0:T(2,128)(2,1)} copy(bf16[2,2,2,16,8,2,128]{6,4,5,1,0,3,2:T(8,128)(2,1)S(1)} %bitcast.5) | data formatting | bytes 1048576 | tf_op jit(solution)/shard_map/transpose | solution.py:465
Async XLA Ops:
  0.0 3.5 %copy-start = (bf16[512,512]{1,0:T(8,128)(2,1)S(1)}, bf16[512,512]{1,0:T(8,128)(2,1)}, u32[]{:S(2)}) copy-start(bf16[512,512]{1,0:T(8,128)(2,1)} %constant.13.low) | copy-start | bytes 1572868
  0.0 3.5 %copy-start.1 = (f32[16,32,128]{2,1,0:T(8,128)S(1)}, f32[16,32,128]{2,1,0:T(8,128)}, u32[]{:S(2)}) copy-start(f32[16,32,128]{2,1,0:T(8,128)} %constant.8.clone.win) | copy-start | bytes 786436
  0.0 3.5 %copy-start.2 = (bf16[256,256]{1,0:T(8,128)(2,1)S(1)}, bf16[256,256]{1,0:T(8,128)(2,1)}, u32[]{:S(2)}) copy-start(bf16[256,256]{1,0:T(8,128)(2,1)} %constant.14.high) | copy-start | bytes 393220
  0.0 3.5 %copy-start.3 = (f32[128,128]{1,0:T(8,128)S(1)}, f32[128,128]{1,0:T(8,128)}, u32[]{:S(2)}) copy-start(f32[128,128]{1,0:T(8,128)} %table.1) | copy-start | bytes 196612
  0.0 3.5 %copy-start.4 = (f32[32,2,256]{2,1,0:T(2,128)S(1)}, f32[32,2,256]{2,1,0:T(2,128)}, u32[]{:S(2)}) copy-start(f32[32,2,256]{2,1,0:T(2,128)} %constant.11.clone.twid) | copy-start | bytes 196612
  0.0 3.5 %copy-start.5 = (s32[32]{0:T(128)S(1)}, s32[32]{0:T(128)}, u32[]{:S(2)}) copy-start(s32[32]{0:T(128)} %pointing.1) | copy-start | bytes 388
  0.0 3.5 %copy-start.6 = (s32[128]{0:T(128)S(1)}, s32[128]{0:T(128)}, u32[]{:S(2)}) copy-start(s32[128]{0:T(128)} %param.11) | copy-start | bytes 1540
